TPU v7x, 128 devices: a whole 4x4x4 slice. The times are simulated.
128 devices in a mesh: dp: 8 (over z, y_hi), expert: 16 (over y_lo, x, core).
Axes of the slice: x: 4, y: 4 (y_hi: 2, y_lo: 2; y = y_hi * 2 + y_lo), z: 4, core: 2. Of those that a mesh axis runs over, the one named last changes fastest.
Arguments:
- tokens: bfloat16 [16384, 2048], P(('dp', 'expert')), may hold values from -6 to 6
- out_grad: bfloat16 [16384, 2048], P(('dp', 'expert')), may hold values from -1.5 to 1.5
- gate_probs: float32 [16384, 2], P(('dp', 'expert')), may hold values from 0.1 to 1
- expert_ids: int32 [16384, 2], P(('dp', 'expert')), may hold values from 0 to 31, all different within a row; in each aligned block of 128 rows (0 to 127, 128 to 255, ...) at most 12 rows name the same one
- gate_weight: bfloat16 [32, 2048, 2048], P('expert', None, 'dp'), may hold values from -0.125 to 0.125
- up_weight: bfloat16 [32, 2048, 2048], P('expert', None, 'dp'), may hold values from -0.125 to 0.125
- down_weight: bfloat16 [32, 2048, 2048], P('expert', 'dp'), may hold values from -0.125 to 0.125
Outputs:
- d_tokens: bfloat16 [16384, 2048], P(('dp', 'expert'))
- grad_gate: float32 [32, 2048, 2048], P('expert', None, 'dp')
- grad_up: float32 [32, 2048, 2048], P('expert', None, 'dp')
- grad_down: float32 [32, 2048, 2048], P('expert', 'dp')
Inputs may be any that keep to these rules, and one draw needn't show every extreme that they name: `expert_ids`: each token names two different experts. Among the 128 tokens of one device no expert is named more than 12 times, a bound that some block reaches there.
All inputs are finite; a program needn't handle non-finite values.
Results may differ from a plain program's by a relative error of at most 0.014.
Values may be sent and summed in bfloat16 or wider, within the bound.
A program may use at most 192 MiB of HBM per device.

v0:
```python
import jax
import jax.numpy as jnp
from jax import lax
from jax.sharding import PartitionSpec as P


def body(tokens, out_grad, gate_probs, expert_ids, gate_weight, up_weight, down_weight):
    columns = lax.axis_size("expert")
    groups = lax.axis_size("dp")
    per_column = gate_weight.shape[0]
    experts = per_column * columns
    width = tokens.shape[1]
    token_count = tokens.shape[0]
    capacity = max(2, 3 * token_count // experts)
    flat_ids = expert_ids.reshape(-1)
    onehot = (flat_ids[:, None] == jnp.arange(experts, dtype=jnp.int32)[None, :]).astype(jnp.int32)
    earlier = jnp.cumsum(onehot, axis=0) - onehot
    position = flat_ids * capacity + jnp.sum(earlier * onehot, axis=1)
    token_rows = jnp.repeat(tokens, 2, axis=0)
    scaled = (
        gate_probs.reshape(-1, 1) * jnp.repeat(out_grad, 2, axis=0).astype(jnp.float32)
    ).astype(jnp.bfloat16)
    send_rows = jnp.zeros((experts * capacity, width), jnp.bfloat16).at[position].set(token_rows)
    send_grads = jnp.zeros((experts * capacity, width), jnp.bfloat16).at[position].set(scaled)
    wide_rows = jnp.broadcast_to(send_rows[None], (groups, experts * capacity, width)).reshape(
        groups * experts * capacity, width
    )
    wide_grads = jnp.broadcast_to(send_grads[None], (groups, experts * capacity, width)).reshape(
        groups * experts * capacity, width
    )
    got_rows, got_grads = (
        lax.all_to_all(wide_rows, ("dp", "expert"), split_axis=0, concat_axis=0, tiled=True),
        lax.all_to_all(wide_grads, ("dp", "expert"), split_axis=0, concat_axis=0, tiled=True),
    )
    sources = groups * columns
    arrived = got_rows.reshape(sources, per_column, capacity, width)
    arrived_grads = got_grads.reshape(sources, per_column, capacity, width)
    gate_pre = jnp.einsum(
        "sjcd,jdh->sjch", arrived, gate_weight, preferred_element_type=jnp.float32
    )
    up_pre = jnp.einsum("sjcd,jdh->sjch", arrived, up_weight, preferred_element_type=jnp.float32)
    gate_sigmoid = jax.nn.sigmoid(gate_pre)
    gate_silu = gate_pre * gate_sigmoid
    hidden_act = (gate_silu * up_pre).astype(jnp.bfloat16)
    hidden_grad = jnp.einsum(
        "sjcd,jhd->sjch", arrived_grads, down_weight, preferred_element_type=jnp.float32
    )
    grad_down = jnp.einsum(
        "sjch,sjcd->jhd", hidden_act, arrived_grads, preferred_element_type=jnp.float32
    )
    gate_grad = (
        hidden_grad * up_pre * gate_sigmoid * (1.0 + gate_pre * (1.0 - gate_sigmoid))
    ).astype(jnp.bfloat16)
    up_grad = (hidden_grad * gate_silu).astype(jnp.bfloat16)
    grad_gate = jnp.einsum("sjcd,sjch->jdh", arrived, gate_grad, preferred_element_type=jnp.float32)
    grad_up = jnp.einsum("sjcd,sjch->jdh", arrived, up_grad, preferred_element_type=jnp.float32)
    partial_value = jnp.einsum(
        "sjch,jdh->sjcd", gate_grad, gate_weight, preferred_element_type=jnp.float32
    )
    partial_value = (
        partial_value
        + jnp.einsum("sjch,jdh->sjcd", up_grad, up_weight, preferred_element_type=jnp.float32)
    ).astype(jnp.bfloat16)
    returned = lax.all_to_all(
        partial_value.reshape(sources * per_column * capacity, width),
        ("dp", "expert"),
        split_axis=0,
        concat_axis=0,
        tiled=True,
    )
    summed = jnp.sum(
        returned.reshape(groups, experts * capacity, width), axis=0, dtype=jnp.float32
    ).astype(jnp.bfloat16)
    slot_rows = summed[position]
    d_tokens = jnp.sum(slot_rows.reshape(token_count, 2, width), axis=1, dtype=jnp.float32).astype(
        jnp.bfloat16
    )
    return (d_tokens, grad_gate, grad_up, grad_down)


def solution(mesh):
    in_specs = (
        P(("dp", "expert"), None),
        P(("dp", "expert"), None),
        P(("dp", "expert"), None),
        P(("dp", "expert"), None),
        P("expert", None, "dp"),
        P("expert", None, "dp"),
        P("expert", "dp", None),
    )
    out_specs = (
        P(("dp", "expert"), None),
        P("expert", None, "dp"),
        P("expert", None, "dp"),
        P("expert", "dp", None),
    )
    return jax.shard_map(body, mesh=mesh, in_specs=in_specs, out_specs=out_specs, check_vma=False)
```

profile of v0, /device:TPU:90, one launch (start us, length us, event | category | flops | bytes accessed | tf_op | source)
XLA Modules:
  0.0 643.1 jit_solution(11205437356169142351)
XLA Ops:
  6.6 4.1 scatter_custom_fusion.1
  10.8 7.6 %broadcast_in_dim.11 = bf16[8,384,2048]{2,1,0:T(8,128)(2,1)} broadcast(bf16[384,2048]{1,0:T(8,128)(2,1)} %scatter_custom_fusion.1), dimensions={1,2} | broadcast | bytes 14155776 | tf_op jit(solution)/shard_map/broadcast_in_dim | solution.py:25
  18.4 10.3 %all-to-all-start.1 = ((bf16[128,24,2048]{2,1,0:T(8,128)(2,1)}), bf16[128,24,2048]{2,1,0:T(8,128)(2,1)}, u32[]{:S(2)}, u32[]{:S(2)}) async-start(bf16[128,24,2048]{2,1,0:T(8,128)(2,1)} %bitcast.117), calls=%async_computation.1 | async-start | bytes 25165824 | tf_op jit(solution)/shard_map/all_to_all | solution.py:32
  34.9 4.5 scatter_custom_fusion
  39.5 158.3 %all-to-all-done.1 = bf16[128,24,2048]{2,1,0:T(8,128)(2,1)} async-done(((bf16[128,24,2048]{2,1,0:T(8,128)(2,1)}), bf16[128,24,2048]{2,1,0:T(8,128)(2,1)}, u32[]{:S(2)}, u32[]{:S(2)}) %all-to-all-start.1) | async-done | bytes 12582944 | tf_op jit(solution)/shard_map/all_to_all | solution.py:32
  197.8 7.5 %broadcast_in_dim.9 = bf16[8,384,2048]{2,1,0:T(8,128)(2,1)} broadcast(bf16[384,2048]{1,0:T(8,128)(2,1)} %scatter_custom_fusion), dimensions={1,2} | broadcast | bytes 14155776 | tf_op jit(solution)/shard_map/broadcast_in_dim | solution.py:28
  205.3 8.8 %all-to-all-start = ((bf16[128,24,2048]{2,1,0:T(8,128)(2,1)}), bf16[128,24,2048]{2,1,0:T(8,128)(2,1)}, u32[]{:S(2)}, u32[]{:S(2)}) async-start(bf16[128,24,2048]{2,1,0:T(8,128)(2,1)} %bitcast.118), calls=%async_computation | async-start | bytes 25165824 | tf_op jit(solution)/shard_map/all_to_all | solution.py:33
  214.0 11.7 %copy.20 = bf16[128,24,2048]{2,0,1:T(8,128)(2,1)S(1)} copy(bf16[128,24,2048]{2,1,0:T(8,128)(2,1)} %all-to-all-done.1) | data formatting | bytes 25165824 | tf_op jit(solution)/shard_map/all_to_all | solution.py:32
  225.8 5.6 fusion.11
  231.6 5.2 fusion.16
  236.8 141.9 %all-to-all-done = bf16[128,24,2048]{2,1,0:T(8,128)(2,1)} async-done(((bf16[128,24,2048]{2,1,0:T(8,128)(2,1)}), bf16[128,24,2048]{2,1,0:T(8,128)(2,1)}, u32[]{:S(2)}, u32[]{:S(2)}) %all-to-all-start) | async-done | bytes 12582944 | tf_op jit(solution)/shard_map/all_to_all | solution.py:33
  378.8 14.8 %copy.19 = bf16[128,24,2048]{2,0,1:T(8,128)(2,1)} copy(bf16[128,24,2048]{2,1,0:T(8,128)(2,1)} %all-to-all-done) | data formatting | bytes 25165824 | tf_op jit(solution)/shard_map/all_to_all | solution.py:33
  393.6 11.5 %fusion.8 = (bf16[128,2,12,256]{3,0,2,1:T(8,128)(2,1)}, bf16[128,2,12,256]{3,0,2,1:T(8,128)(2,1)S(1)}) fusion(f32[2,128,12,256]{3,1,2,0:T(8,128)S(1)} %copy-done.9, f32[2,128,12,256]{3,1,2,0:T(8,128)} %fusion.16, bf16[128,2,12,2048]{3,0,2,1:T(8,128)(2,1)} %bitcast.124, bf16[2,256,2048]{2,1,0:T(8,128)(2,1)S(1)} %copy-done.8), kind=kOutput, calls=%fused_computation.22 | convolution fusion | flops 3231449088 | bytes 24117248 | tf_op jit(solution)/shard_map/sjcd,jhd->sjch/dot_general | solution.py:45
  405.1 10.1 %fusion.9 = f32[2,128,12,2048]{3,1,2,0:T(8,128)} fusion(bf16[128,2,12,256]{3,0,2,1:T(8,128)(2,1)S(1)} %get-tuple-element.5, bf16[2,2048,256]{2,1,0:T(8,128)(2,1)S(1)} %copy-done), kind=kOutput, calls=%fused_computation.23 | convolution fusion | flops 3221225472 | bytes 28835840 | tf_op jit(solution)/shard_map/sjch,jdh->sjcd/dot_general | solution.py:57
  415.2 16.0 %add_convert_fusion = bf16[2,128,12,2048]{3,1,2,0:T(8,128)(2,1)} fusion(f32[2,128,12,2048]{3,1,2,0:T(8,128)} %fusion.9, bf16[128,2,12,256]{3,0,2,1:T(8,128)(2,1)} %get-tuple-element.4, bf16[2,2048,256]{2,1,0:T(8,128)(2,1)} %param.12), kind=kOutput, calls=%fused_computation.3 | convolution fusion | flops 3233808384 | bytes 41418752 | tf_op jit(solution)/shard_map/sjch,jdh->sjcd/dot_general | solution.py:62
  431.2 14.5 %copy.21 = bf16[128,24,2048]{2,1,0:T(8,128)(2,1)} copy(bf16[128,24,2048]{2,0,1:T(8,128)(2,1)} %bitcast.119) | data formatting | bytes 25165824 | tf_op jit(solution)/shard_map/all_to_all | solution.py:64
  445.7 9.1 %all-to-all-start.2 = ((bf16[128,24,2048]{2,1,0:T(8,128)(2,1)}), bf16[128,24,2048]{2,1,0:T(8,128)(2,1)}, u32[]{:S(2)}, u32[]{:S(2)}) async-start(bf16[128,24,2048]{2,1,0:T(8,128)(2,1)} %copy.21), calls=%async_computation.2 | async-start | bytes 25165824 | tf_op jit(solution)/shard_map/all_to_all | solution.py:64
  454.9 12.1 %convolution_bitcast_fusion.1 = f32[2,2048,256]{2,1,0:T(8,128)} fusion(bf16[128,2,12,2048]{3,0,2,1:T(8,128)(2,1)} %bitcast.122, bf16[128,2,12,256]{3,0,2,1:T(8,128)(2,1)} %get-tuple-element.4), kind=kOutput, calls=%fused_computation.6 | convolution fusion | flops 3221225472 | bytes 18350080 | tf_op jit(solution)/shard_map/sjcd,sjch->jdh/dot_general | solution.py:56
  467.0 11.6 %convolution_bitcast_fusion.2 = f32[2,2048,256]{2,1,0:T(8,128)} fusion(bf16[128,2,12,2048]{3,0,2,1:T(8,128)(2,1)} %bitcast.123, bf16[128,2,12,256]{3,0,2,1:T(8,128)(2,1)S(1)} %copy-done.5), kind=kOutput, calls=%fused_computation.7 | convolution fusion | flops 3221225472 | bytes 18350080 | tf_op jit(solution)/shard_map/sjcd,sjch->jdh/dot_general | solution.py:55
  478.6 12.1 %convolution_bitcast_fusion = f32[2,256,2048]{2,1,0:T(8,128)} fusion(bf16[128,2,12,2048]{3,0,2,1:T(8,128)(2,1)} %bitcast.125, f32[2,128,12,256]{3,1,2,0:T(8,128)} %fusion.16, f32[2,128,12,256]{3,1,2,0:T(8,128)} %fusion.11), kind=kOutput, calls=%fused_computation.5 | convolution fusion | flops 3225944064 | bytes 23068672 | tf_op jit(solution)/shard_map/sjch,sjcd->jhd/dot_general | solution.py:48
  490.7 132.8 %all-to-all-done.2 = bf16[128,24,2048]{2,1,0:T(8,128)(2,1)} async-done(((bf16[128,24,2048]{2,1,0:T(8,128)(2,1)}), bf16[128,24,2048]{2,1,0:T(8,128)(2,1)}, u32[]{:S(2)}, u32[]{:S(2)}) %all-to-all-start.2) | async-done | bytes 12582944 | tf_op jit(solution)/shard_map/all_to_all | solution.py:64
  623.5 9.1 %bitcast_reduce_fusion = bf16[384,2048]{1,0:T(8,128)(2,1)} fusion(bf16[8,384,2048]{2,1,0:T(8,128)(2,1)} %bitcast.114), kind=kLoop, calls=%fused_computation.4 | loop fusion | flops 5505024 | bytes 14155776 | tf_op jit(solution)/shard_map/reduce_sum | solution.py:71
  632.7 4.1 gather_fusion
  638.3 4.6 reduce_sum.38
  (41 shorter events, 14.1 us)
Async XLA Ops:
  0.6 225.1 %copy-start = (bf16[2,2048,256]{2,1,0:T(8,128)(2,1)S(1)}, bf16[2,2048,256]{2,1,0:T(8,128)(2,1)}, u32[]{:S(2)}) copy-start(bf16[2,2048,256]{2,1,0:T(8,128)(2,1)} %param.11) | copy-start | bytes 6291460
  18.4 10.3 %copy-start.7 = (f32[128,2]{0,1:T(2,128)S(1)}, f32[128,2]{0,1:T(2,128)}, u32[]{:S(2)}) copy-start(f32[128,2]{0,1:T(2,128)} %param.9) | copy-start | bytes 3076
  18.4 10.6 %copy-start.6 = (bf16[128,2048]{1,0:T(8,128)(2,1)S(1)}, bf16[128,2048]{1,0:T(8,128)(2,1)}, u32[]{:S(2)}) copy-start(bf16[128,2048]{1,0:T(8,128)(2,1)} %param.8) | copy-start | bytes 1572868
  18.4 179.4 %all-to-all-start.1 = ((bf16[128,24,2048]{2,1,0:T(8,128)(2,1)}), bf16[128,24,2048]{2,1,0:T(8,128)(2,1)}, u32[]{:S(2)}, u32[]{:S(2)}) async-start(bf16[128,24,2048]{2,1,0:T(8,128)(2,1)} %bitcast.117), calls=%async_computation.1 | async-start | bytes 25165824 | tf_op jit(solution)/shard_map/all_to_all | solution.py:32
  205.3 173.5 %all-to-all-start = ((bf16[128,24,2048]{2,1,0:T(8,128)(2,1)}), bf16[128,24,2048]{2,1,0:T(8,128)(2,1)}, u32[]{:S(2)}, u32[]{:S(2)}) async-start(bf16[128,24,2048]{2,1,0:T(8,128)(2,1)} %bitcast.118), calls=%async_computation | async-start | bytes 25165824 | tf_op jit(solution)/shard_map/all_to_all | solution.py:33
  225.7 5.9 copy-start.2
  225.7 5.9 copy-start.3
  378.8 14.8 %copy-start.8 = (bf16[2,256,2048]{2,1,0:T(8,128)(2,1)S(1)}, bf16[2,256,2048]{2,1,0:T(8,128)(2,1)}, u32[]{:S(2)}) copy-start(bf16[2,256,2048]{2,1,0:T(8,128)(2,1)} %param.13) | copy-start | bytes 6291460
  378.8 14.8 %copy-start.9 = (f32[2,128,12,256]{3,1,2,0:T(8,128)S(1)}, f32[2,128,12,256]{3,1,2,0:T(8,128)}, u32[]{:S(2)}) copy-start(f32[2,128,12,256]{3,1,2,0:T(8,128)} %fusion.11) | copy-start | bytes 9437188
  405.1 10.1 %copy-start.4 = (bf16[128,2,12,256]{3,0,2,1:T(8,128)(2,1)}, bf16[128,2,12,256]{3,0,2,1:T(8,128)(2,1)S(1)}, u32[]{:S(2)}) copy-start(bf16[128,2,12,256]{3,0,2,1:T(8,128)(2,1)S(1)} %get-tuple-element.5) | copy-start | bytes 4718596
  445.7 177.8 %all-to-all-start.2 = ((bf16[128,24,2048]{2,1,0:T(8,128)(2,1)}), bf16[128,24,2048]{2,1,0:T(8,128)(2,1)}, u32[]{:S(2)}, u32[]{:S(2)}) async-start(bf16[128,24,2048]{2,1,0:T(8,128)(2,1)} %copy.21), calls=%async_computation.2 | async-start | bytes 25165824 | tf_op jit(solution)/shard_map/all_to_all | solution.py:64
  454.9 12.1 %copy-start.5 = (bf16[128,2,12,256]{3,0,2,1:T(8,128)(2,1)S(1)}, bf16[128,2,12,256]{3,0,2,1:T(8,128)(2,1)}, u32[]{:S(2)}) copy-start(bf16[128,2,12,256]{3,0,2,1:T(8,128)(2,1)} %copy-done.4) | copy-start | bytes 4718596
  632.7 10.2 %copy-start.1 = (bf16[2,2048,256]{2,1,0:T(8,128)(2,1)S(1)}, bf16[2,2048,256]{2,1,0:T(8,128)(2,1)}, u32[]{:S(2)}) copy-start(bf16[2,2048,256]{2,1,0:T(8,128)(2,1)} %param.11) | copy-start | bytes 6291460
where the time goes:
time: 652 us; the launch traced here: 643 us
  waiting for transfers between devices  433 us (66%)
  matrix products  84.2 us (13%)
  local copies, waits for them, and re-layouts  76.9 us (12%)
  starting transfers between devices  28.2 us (4%)
  other arithmetic  19.8 us (3%)
    all_to_all x1, waiting for transfers between devices, body(): lax.all_to_all(wide_rows, ('dp', 'expert'), split_axis=0, concat_axis=0,...  158 us
    all_to_all x1, waiting for transfers between devices, body(): lax.all_to_all(wide_grads, ('dp', 'expert'), split_axis=0, concat_axis=0,...  142 us
    all_to_all x1, waiting for transfers between devices, body(): lax.all_to_all(partial_value.reshape(sources * per_column * capacity, wid...  133 us
    dot_general x1, matrix products, body(): jnp.einsum('sjch,jdh->sjcd', up_grad, up_weight, preferred_element_type=j...  16 us
    all_to_all x1, local copies, waits for them, and re-layouts, body(): lax.all_to_all(wide_grads, ('dp', 'expert'), split_axis=0, concat_axis=0,...  14.8 us
    all_to_all x1, local copies, waits for them, and re-layouts, body(): lax.all_to_all(partial_value.reshape(sources * per_column * capacity, wid...  14.5 us
  transfers between devices with their start and end apart: 3, of which 3 were waited for; matrix products, arithmetic and copies ran while one was open for 11% of the time, Pallas kernels for 0%

commit v1 on v0

v1 whole, which is shorter than its diff:
```python
import jax
import jax.numpy as jnp
from jax import lax
from jax.experimental import pallas as pl
from jax.experimental.pallas import tpu as pltpu
from jax.sharding import PartitionSpec as P

MESH = pl.DeviceIdType.MESH
BF = jnp.bfloat16
F32 = jnp.float32
CAP = 12
MSG = 4 * CAP
BLK = 4 * MSG
HALF = 4 * BLK
ROWS = 8 * BLK
WIDE = 512
AT = ((1,), (0,))
TB = ((1,), (1,))
TA = ((0,), (0,))


def dot(a, b, dims):
    return lax.dot_general(a, b, (dims, ((), ())), preferred_element_type=F32)


def place():
    dp, ex = lax.axis_index("dp"), lax.axis_index("expert")
    return lax.rem(lax.div(ex, 2), 4), lax.rem(dp, 2) * 2 + lax.div(ex, 8), lax.div(dp, 2), lax.rem(ex, 2)


def device(x, y, z, c):
    return (z * 2 + lax.div(y, 2), lax.rem(y, 2) * 8 + x * 2 + c)


def kernel(
    tokens, out_grad, meta_in, wg_hbm, wu_hbm, wd_hbm,
    d_out, gg_out, gu_out, gd_out, near, above, below, opp, ret_a, ret_b, back, back_o,
    both, far, meta, far_meta, msg, msg_o, perm, stage, tok, grad, hid, part, p_near, p_above, p_below, p_opp,
    rstage, dacc, dsend, dfar, wg, wu, wd, ag, au, ad,
    far_s, far_r, loc, near_s, near_r, opp_s, opp_r, fwd_s, above_r, below_r, pa_s, ret_s, reta_r, retb_r,
    back_s, back_r, backo_s, backo_r, dfar_s, dfar_r, st_s, out_s,
):
    x, y, z, c = place()
    up = device(x, y, lax.rem(z + 1, 4), c)
    down = device(x, y, lax.rem(z + 3, 4), c)
    over = device(x, y, lax.rem(z + 2, 4), c)

    def peer(k, dx, sign):
        dy, dc = lax.div(k, 2), lax.rem(k, 2)
        return device(lax.rem(x + sign * dx + 4, 4), lax.rem(y + sign * dy + 4, 4), z, lax.rem(c + dc, 2))

    loads = [
        pltpu.make_async_copy(tokens, both.at[pl.ds(0, 128)], loc.at[0]),
        pltpu.make_async_copy(out_grad, both.at[pl.ds(128, 128)], loc.at[1]),
        pltpu.make_async_copy(wg_hbm, wg, loc.at[2]),
        pltpu.make_async_copy(wu_hbm, wu, loc.at[3]),
        pltpu.make_async_copy(wd_hbm, wd, loc.at[4]),
    ]
    for cp in loads:
        cp.start()

    barrier = pltpu.get_barrier_semaphore()
    for other in (up, down, over):
        pl.semaphore_signal(barrier, inc=1, device_id=other, device_id_type=MESH)

    def greet(s, _):
        pl.semaphore_signal(barrier, inc=1, device_id=peer(lax.div(s, 4), lax.rem(s, 4), 1), device_id_type=MESH)
        return 0

    lax.fori_loop(1, 32, greet, 0)

    e0, e1 = meta_in[0:1, :], meta_in[1:2, :]
    ei = lax.broadcasted_iota(jnp.int32, (32, 128), 0).astype(F32)
    h0, h1 = ei == e0, ei == e1
    before = (lax.broadcasted_iota(jnp.int32, (128, 128), 0) < lax.broadcasted_iota(jnp.int32, (128, 128), 1))
    counts = jnp.where(h0 | h1, 1.0, 0.0).astype(BF)
    earlier = dot(counts, jnp.where(before, 1.0, 0.0).astype(BF), AT)

    def row_of(hit, e):
        slot = jnp.sum(jnp.where(hit, earlier, 0.0), axis=0, keepdims=True)
        return 24.0 * e - 12.0 * (e - 2.0 * jnp.floor(e * 0.5)) + slot

    meta[0:1, :] = row_of(h0, e0)
    meta[1:2, :] = row_of(h1, e1)
    meta[2:4, :] = meta_in[2:4, :]
    meta[4:8, :] = meta_in[4:8, :]

    ri = lax.broadcasted_iota(jnp.int32, (BLK, BLK), 0)
    ci = lax.broadcasted_iota(jnp.int32, (BLK, BLK), 1)
    src = lax.div(lax.rem(ri, MSG), CAP) * MSG + lax.div(ri, MSG) * CAP + lax.rem(ri, CAP)
    perm[...] = jnp.where(ci == src, 1.0, 0.0).astype(BF)

    pl.semaphore_wait(barrier, 34)
    fars = [
        pltpu.make_async_remote_copy(tokens, far.at[pl.ds(0, 128)], far_s.at[0], far_r.at[0], device_id=over, device_id_type=MESH),
        pltpu.make_async_remote_copy(out_grad, far.at[pl.ds(128, 128)], far_s.at[1], far_r.at[1], device_id=over, device_id_type=MESH),
        pltpu.make_async_remote_copy(meta, far_meta, far_s.at[2], far_r.at[2], device_id=over, device_id_type=MESH),
    ]
    for cp in fars:
        cp.start()

    def rows_of(k):
        dy, dc = lax.div(k, 2), lax.rem(k, 2)
        r = lax.broadcasted_iota(jnp.int32, (BLK, 1), 0)
        q = lax.rem(r, MSG)
        column = lax.rem(y + dy, 2) * 8 + lax.rem(x + lax.div(r, MSG), 4) * 2 + lax.rem(c + dc, 2)
        return (column * MSG + q).astype(F32), q

    def build(rows, m, out, g):
        want, q = rows_of(g)
        t0, t1, p0, p1 = m[0:1, :], m[1:2, :], m[2:3, :], m[3:4, :]
        hit_t = (want == t0) | (want == t1)
        hit0, hit1 = want - 24.0 == t0, want - 24.0 == t1
        hit_t = jnp.where(q < 24, jnp.where(hit_t, 1.0, 0.0), 0.0)
        hit0 = jnp.where(q >= 24, jnp.where(hit0, 1.0, 0.0), 0.0)
        hit1 = jnp.where(q >= 24, jnp.where(hit1, 1.0, 0.0), 0.0)
        pick = jnp.concatenate([hit_t, hit0 + hit1], axis=1).astype(BF)
        scale = jnp.sum(hit0 * p0 + hit1 * p1, axis=1, keepdims=True) + jnp.where(q < 24, 1.0, 0.0)
        base = pl.multiple_of(g * BLK, BLK)

        def part_of(n, _):
            cols = pl.ds(pl.multiple_of(n * WIDE, WIDE), WIDE)
            out[pl.ds(base, BLK), cols] = (dot(pick, rows[:, cols], AT) * scale).astype(BF)
            return 0

        lax.fori_loop(0, 2048 // WIDE, part_of, 0)

    def send_block(k, src_buf, dst_buf, ssem, rsem, base, sign, width):
        for dx in range(4):
            frm = src_buf.at[pl.ds(pl.multiple_of(base + dx * MSG, MSG), MSG), pl.ds(0, width)]
            to = dst_buf.at[pl.ds(pl.multiple_of(k * BLK + dx * MSG, MSG), MSG), pl.ds(0, width)]
            if dx == 0:
                @pl.when(k == 0)
                def _():
                    pltpu.make_async_copy(frm, to, rsem.at[k]).start()

                @pl.when(k > 0)
                def _():
                    pltpu.make_async_remote_copy(frm, to, ssem.at[0], rsem.at[k], device_id=peer(k, dx, sign), device_id_type=MESH).start()
            else:
                pltpu.make_async_remote_copy(frm, to, ssem.at[0], rsem.at[k], device_id=peer(k, dx, sign), device_id_type=MESH).start()

    def block(ref, k):
        return ref.at[pl.ds(pl.multiple_of(k * BLK, BLK), BLK)]

    def got(ref, k, sem):
        pltpu.make_async_copy(block(ref, k), block(ref, k), sem.at[k]).wait()

    loads[0].wait()
    loads[1].wait()

    def dispatch(rows, m, out, dst, ssem, rsem):
        def one(g, _):
            build(rows, m, out, g)
            base = g * BLK
            send_block(g, out, dst, ssem, rsem, base, 1, 2048)
            send_block(g + 4, out, dst, ssem, rsem, base, 1, 2048)
            return 0

        lax.fori_loop(0, 4, one, 0)

    dispatch(both, meta, msg, near, near_s, near_r)

    def clear(n, _):
        rows = pl.ds(pl.multiple_of(n * 256, 256), 256)
        for e in range(2):
            ag[e, rows, :] = jnp.zeros((256, 256), F32)
            au[e, rows, :] = jnp.zeros((256, 256), F32)
        return 0

    lax.fori_loop(0, 8, clear, 0)

    def clear_d(n, _):
        cols = pl.ds(pl.multiple_of(n * 256, 256), 256)
        for e in range(2):
            ad[e, :, cols] = jnp.zeros((256, 256), F32)
        return 0

    lax.fori_loop(0, 8, clear_d, 0)
    for cp in loads[2:]:
        cp.wait()

    def forward(k, _):
        got(near, k, near_r)
        pltpu.make_async_remote_copy(block(near, k), block(below, k), fwd_s.at[0], below_r.at[k], device_id=up, device_id_type=MESH).start()
        pltpu.make_async_remote_copy(block(near, k), block(above, k), fwd_s.at[1], above_r.at[k], device_id=down, device_id_type=MESH).start()
        return 0

    def half(ref, h):
        return ref.at[pl.ds(h * HALF, HALF)]

    def load(buf, h):
        return pltpu.make_async_copy(half(buf, h), stage, st_s.at[0])

    def compute(buf, h, out):
        cp = load(buf, h)
        cp.start()
        cp.wait()

        def sort_in(i, _):
            b, n = lax.div(i, 4), lax.rem(i, 4)
            cols = pl.ds(pl.multiple_of(n * WIDE, WIDE), WIDE)
            v = dot(perm[...], stage[pl.ds(pl.multiple_of(b * BLK, BLK), BLK), cols], AT).astype(BF)
            rows = pl.ds(pl.multiple_of(b * MSG, MSG), MSG)
            tok[0, rows, cols] = v[0:48]
            tok[1, rows, cols] = v[48:96]
            grad[0, rows, cols] = v[96:144]
            grad[1, rows, cols] = v[144:192]
            return 0

        lax.fori_loop(0, 16, sort_in, 0)

        def expert(e, _):
            gate = dot(tok[e], wg[e], AT)
            upv = dot(tok[e], wu[e], AT)
            hg = dot(grad[e], wd[e], TB)
            s = jax.nn.sigmoid(gate)
            silu = gate * s
            hid[0] = (silu * upv).astype(BF)
            hid[1] = (hg * upv * s * (1.0 + gate * (1.0 - s))).astype(BF)
            hid[2] = (hg * silu).astype(BF)

            def tile(n, _):
                cols = pl.ds(pl.multiple_of(n * WIDE, WIDE), WIDE)
                part[e, :, cols] = (dot(hid[1], wg[e, cols, :], TB) + dot(hid[2], wu[e, cols, :], TB)).astype(BF)
                ag[e, cols, :] += dot(tok[e, :, cols], hid[1], TA)
                au[e, cols, :] += dot(tok[e, :, cols], hid[2], TA)
                ad[e, :, cols] += dot(hid[0], grad[e, :, cols], TA)
                return 0

            lax.fori_loop(0, 2048 // WIDE, tile, 0)
            return 0

        lax.fori_loop(0, 2, expert, 0)

        def sort_out(i, _):
            b, n = lax.div(i, 2), lax.rem(i, 2)
            rows = pl.ds(pl.multiple_of(b * MSG, MSG), MSG)
            lo = pl.ds(pl.multiple_of(n * WIDE, WIDE), WIDE)
            hi = pl.ds(pl.multiple_of(n * WIDE + 1024, WIDE), WIDE)
            v = jnp.concatenate([part[0, rows, lo], part[1, rows, lo], part[0, rows, hi], part[1, rows, hi]], axis=0)
            out[pl.ds(pl.multiple_of(h * HALF + b * BLK, BLK), BLK), lo] = dot(perm[...], v, AT).astype(BF)
            return 0

        lax.fori_loop(0, 8, sort_out, 0)

    def got_half(ref, h, sem):
        def one(k, _):
            got(ref, k, sem)
            return 0

        lax.fori_loop(4 * h, 4 * h + 4, one, 0)

    def give(h):
        def one(k, _):
            pltpu.make_async_remote_copy(block(p_below, k), block(ret_a, k), ret_s.at[0], reta_r.at[k], device_id=down, device_id_type=MESH).start()
            pltpu.make_async_remote_copy(block(p_above, k), block(ret_b, k), ret_s.at[1], retb_r.at[k], device_id=up, device_id_type=MESH).start()
            return 0

        lax.fori_loop(4 * h, 4 * h + 4, one, 0)

    def settle(h):
        def one(k, _):
            got(ret_a, k, reta_r)
            got(ret_b, k, retb_r)
            ca = pltpu.make_async_copy(block(ret_a, k), rstage.at[pl.ds(0, BLK)], st_s.at[1])
            cb = pltpu.make_async_copy(block(ret_b, k), rstage.at[pl.ds(BLK, BLK)], st_s.at[2])
            ca.start()
            cb.start()
            ca.wait()
            cb.wait()
            rows = pl.ds(pl.multiple_of(k * BLK, BLK), BLK)
            p_near[rows, :] = (p_near[rows, :].astype(F32) + rstage[0:BLK, :].astype(F32) + rstage[BLK : 2 * BLK, :].astype(F32)).astype(BF)
            send_block(k, p_near, back, back_s, back_r, k * BLK, -1, 1024)
            return 0

        lax.fori_loop(4 * h, 4 * h + 4, one, 0)

    def combine(buf, sem, m):
        dacc[...] = jnp.zeros_like(dacc)

        def one(k, _):
            got(buf, k, sem)
            cp = pltpu.make_async_copy(block(buf, k), rstage.at[pl.ds(0, BLK)], st_s.at[1])
            cp.start()
            want, q = rows_of(k)
            t0, t1 = m[0:1, :], m[1:2, :]
            lo = jnp.where(q < 24, jnp.where((want == t0) | (want == t1), 1.0, 0.0), 0.0).astype(BF)
            hi = jnp.where(q >= 24, jnp.where((want - 24.0 == t0) | (want - 24.0 == t1), 1.0, 0.0), 0.0).astype(BF)
            cp.wait()
            dacc[:, 0:1024] += dot(lo, rstage[0:BLK, :], TA)
            dacc[:, 1024:2048] += dot(hi, rstage[0:BLK, :], TA)
            return 0

        lax.fori_loop(0, 8, one, 0)

    lax.fori_loop(0, 4, forward, 0)
    compute(near, 0, p_near)
    lax.fori_loop(4, 8, forward, 0)
    for cp in fars:
        cp.wait()
    dispatch(far, far_meta, msg_o, opp, opp_s, opp_r)
    compute(near, 1, p_near)

    got_half(below, 0, below_r)
    compute(below, 0, p_below)
    got_half(above, 0, above_r)
    compute(above, 0, p_above)
    give(0)

    def send_opp(k, _):
        send_block(k, p_opp, back_o, backo_s, backo_r, k * BLK, -1, 1024)
        return 0

    for h in range(2):
        got_half(opp, h, opp_r)
        compute(opp, h, p_opp)
        lax.fori_loop(4 * h, 4 * h + 4, send_opp, 0)

    got_half(below, 1, below_r)
    compute(below, 1, p_below)
    got_half(above, 1, above_r)
    compute(above, 1, p_above)
    give(1)

    outs = [
        pltpu.make_async_copy(ag, gg_out, out_s.at[0]),
        pltpu.make_async_copy(au, gu_out, out_s.at[1]),
        pltpu.make_async_copy(ad, gd_out, out_s.at[2]),
    ]
    for cp in outs:
        cp.start()

    settle(0)
    combine(back_o, backo_r, far_meta)
    dsend[...] = dacc[...].astype(BF)
    home = pltpu.make_async_remote_copy(dsend, dfar, dfar_s.at[0], dfar_r.at[0], device_id=over, device_id_type=MESH)
    home.start()
    settle(1)
    combine(back, back_r, meta)
    home.wait()
    dacc[...] = dacc[...] + dfar[...].astype(F32)
    dsend[...] = dacc[...].astype(BF)
    last = pltpu.make_async_copy(dsend, d_out, out_s.at[3])
    last.start()

    def sent(ref, rows, sem, i):
        pltpu.make_async_copy(ref.at[pl.ds(0, rows)], ref.at[pl.ds(0, rows)], sem.at[i]).wait()

    sent(near, 31 * MSG, near_s, 0)
    sent(opp, 31 * MSG, opp_s, 0)
    sent(near, ROWS, fwd_s, 0)
    sent(near, ROWS, fwd_s, 1)
    sent(ret_a, ROWS, ret_s, 0)
    sent(ret_b, ROWS, ret_s, 1)
    sent(back, 31 * MSG, back_s, 0)
    sent(back_o, 31 * MSG, backo_s, 0)
    for cp in outs:
        cp.wait()
    last.wait()


def body(tokens, out_grad, probs, ids, wg, wu, wd):
    meta = jnp.concatenate([ids.T.astype(F32), probs.T, jnp.zeros((4, 128), F32)], axis=0)
    hbm = pl.BlockSpec(memory_space=pltpu.HBM)
    vm = pl.BlockSpec(memory_space=pltpu.VMEM)
    sd = jax.ShapeDtypeStruct
    wide, slim = sd((ROWS, 2048), BF), sd((ROWS, 1024), BF)
    dma = pltpu.SemaphoreType.DMA
    outs = pl.pallas_call(
        kernel,
        name="expert_backward",
        out_shape=[
            sd((128, 2048), BF), sd((2, 2048, 256), F32), sd((2, 2048, 256), F32), sd((2, 256, 2048), F32),
            wide, wide, wide, wide, slim, slim, slim, slim,
        ],
        in_specs=[hbm, hbm, vm, hbm, hbm, hbm],
        out_specs=[hbm] * 12,
        scratch_shapes=[
            pltpu.VMEM((256, 2048), BF), pltpu.VMEM((256, 2048), BF), pltpu.VMEM((8, 128), F32), pltpu.VMEM((8, 128), F32),
            pltpu.VMEM((4 * BLK, 2048), BF), pltpu.VMEM((4 * BLK, 2048), BF), pltpu.VMEM((BLK, BLK), BF),
            pltpu.VMEM((HALF, 2048), BF), pltpu.VMEM((2, BLK, 2048), BF), pltpu.VMEM((2, BLK, 2048), BF),
            pltpu.VMEM((3, BLK, 256), BF), pltpu.VMEM((2, BLK, 2048), BF),
            pltpu.VMEM((ROWS, 1024), BF), pltpu.VMEM((ROWS, 1024), BF), pltpu.VMEM((ROWS, 1024), BF), pltpu.VMEM((ROWS, 1024), BF),
            pltpu.VMEM((2 * BLK, 1024), BF), pltpu.VMEM((128, 2048), F32), pltpu.VMEM((128, 2048), BF), pltpu.VMEM((128, 2048), BF),
            pltpu.VMEM((2, 2048, 256), BF), pltpu.VMEM((2, 2048, 256), BF), pltpu.VMEM((2, 256, 2048), BF),
            pltpu.VMEM((2, 2048, 256), F32), pltpu.VMEM((2, 2048, 256), F32), pltpu.VMEM((2, 256, 2048), F32),
            dma((3,)), dma((3,)), dma((5,)), dma((1,)), dma((8,)), dma((1,)), dma((8,)), dma((2,)), dma((8,)), dma((8,)),
            dma((1,)), dma((2,)), dma((8,)), dma((8,)), dma((1,)), dma((8,)), dma((1,)), dma((8,)), dma((1,)), dma((1,)),
            dma((3,)), dma((4,)),
        ],
        compiler_params=pltpu.CompilerParams(collective_id=0, has_side_effects=True, vmem_limit_bytes=62 * 2**20),
    )(tokens, out_grad, meta, wg, wu, wd)
    return tuple(outs[:4])


def solution(mesh):
    tok = P(("dp", "expert"), None)
    col, row = P("expert", None, "dp"), P("expert", "dp", None)
    return jax.shard_map(
        body, mesh=mesh, in_specs=(tok, tok, tok, tok, col, col, row), out_specs=(tok, col, col, row), check_vma=False
    )
```

time: 652 us -> 314 us (0.48)
  the two profiles are of different devices: /device:TPU:90 before, /device:TPU:1 now
where the time goes in v1:
time: 314 us; the launch traced here: 310 us
  Pallas kernels  295 us (94%)
  local copies, waits for them, and re-layouts  12.3 us (4%)
    pallas_call x1, Pallas kernels, body(): pl.pallas_call(kernel, name='expert_backward', out_shape=[sd((128, 2048),...  295 us
    unnamed x8, local copies, waits for them, and re-layouts  12.2 us

profile of v1, /device:TPU:1, one launch (start us, length us, event | category | flops | bytes accessed | tf_op | source)
XLA Modules:
  0.0 310.0 jit_solution(3248167221759418227)
XLA Ops:
  0.6 0.1 pad.2.clone
  0.7 0.7 convert_bitcast_fusion
  1.4 1.3 maximum_maximum_fusion.meta_in
  2.7 295.0 %expert_backward.1 = (bf16[128,2048]{1,0:T(8,128)(2,1)}, f32[2,2048,256]{2,1,0:T(8,128)}, f32[2,2048,256]{2,1,0:T(8,128)}, f32[2,256,2048]{2,1,0:T(8,128)}, bf16...) custom-call(bf16[128,2048]{1,0:T(8,128)(2,1)} %tokens.1, ...), custom_call_target="tpu_custom_call" | custom-call | tf_op jit(solution)/shard_map/expert_backward/pallas_call | solution.py:370
  297.7 1.9 copy.15
  299.6 0.0 copy-start.1
  299.6 4.6 %copy.16 = f32[2,2048,256]{2,1,0:T(8,128)} copy(f32[2,2048,256]{2,1,0:T(8,128)} %get-tuple-element.17) | data formatting | bytes 8388608
  304.2 0.0 copy-done.1
  304.2 0.0 copy-start
  304.2 2.1 copy.17
  306.4 1.6 copy-done
  307.9 2.0 copy.18
  (1 shorter events, 0.0 us)
Async XLA Ops:
  299.6 4.6 %copy-start.1 = (f32[2,2048,256]{2,1,0:T(8,128)S(1)}, f32[2,2048,256]{2,1,0:T(8,128)}, u32[]{:S(2)}) copy-start(f32[2,2048,256]{2,1,0:T(8,128)} %get-tuple-element.18) | copy-start | bytes 12582916
  304.2 3.7 %copy-start = (f32[2,256,2048]{2,1,0:T(8,128)S(1)}, f32[2,256,2048]{2,1,0:T(8,128)}, u32[]{:S(2)}) copy-start(f32[2,256,2048]{2,1,0:T(8,128)} %get-tuple-element.19) | copy-start | bytes 12582916

commit v2 on v1

--- a/solution.py
+++ b/solution.py
@@ -1,3 +1,5 @@
+import functools
+
 import jax
 import jax.numpy as jnp
 from jax import lax
@@ -35,10 +37,10 @@
 def kernel(
     tokens, out_grad, meta_in, wg_hbm, wu_hbm, wd_hbm,
     d_out, gg_out, gu_out, gd_out, near, above, below, opp, ret_a, ret_b, back, back_o,
-    both, far, meta, far_meta, msg, msg_o, perm, stage, tok, grad, hid, part, p_near, p_above, p_below, p_opp,
-    rstage, dacc, dsend, dfar, wg, wu, wd, ag, au, ad,
+    both, far, meta, far_meta, msg, msg_o, perm, stage, tok, grad, act, hid, part, p_near, p_above, p_below, p_opp,
+    rstage, dacc, dsend, dfar, wgu, wd, agu, ad, dout,
     far_s, far_r, loc, near_s, near_r, opp_s, opp_r, fwd_s, above_r, below_r, pa_s, ret_s, reta_r, retb_r,
-    back_s, back_r, backo_s, backo_r, dfar_s, dfar_r, st_s, out_s,
+    back_s, back_r, backo_s, backo_r, dfar_s, dfar_r, st_s, out_s, stage_s,
 ):
     x, y, z, c = place()
     up = device(x, y, lax.rem(z + 1, 4), c)
@@ -46,14 +48,14 @@
     over = device(x, y, lax.rem(z + 2, 4), c)
 
     def peer(k, dx, sign):
-        dy, dc = lax.div(k, 2), lax.rem(k, 2)
+        dy, dc = lax.rem(lax.div(k, 2) + dx, 4), lax.rem(k, 2)
         return device(lax.rem(x + sign * dx + 4, 4), lax.rem(y + sign * dy + 4, 4), z, lax.rem(c + dc, 2))
 
     loads = [
         pltpu.make_async_copy(tokens, both.at[pl.ds(0, 128)], loc.at[0]),
         pltpu.make_async_copy(out_grad, both.at[pl.ds(128, 128)], loc.at[1]),
-        pltpu.make_async_copy(wg_hbm, wg, loc.at[2]),
-        pltpu.make_async_copy(wu_hbm, wu, loc.at[3]),
+        pltpu.make_async_copy(wg_hbm, wgu.at[:, :, pl.ds(0, 256)], loc.at[2]),
+        pltpu.make_async_copy(wu_hbm, wgu.at[:, :, pl.ds(256, 256)], loc.at[3]),
         pltpu.make_async_copy(wd_hbm, wd, loc.at[4]),
     ]
     for cp in loads:
@@ -100,10 +102,9 @@
         cp.start()
 
     def rows_of(k):
-        dy, dc = lax.div(k, 2), lax.rem(k, 2)
         r = lax.broadcasted_iota(jnp.int32, (BLK, 1), 0)
-        q = lax.rem(r, MSG)
-        column = lax.rem(y + dy, 2) * 8 + lax.rem(x + lax.div(r, MSG), 4) * 2 + lax.rem(c + dc, 2)
+        q, dx = lax.rem(r, MSG), lax.div(r, MSG)
+        column = lax.rem(y + lax.div(k, 2) + dx, 2) * 8 + lax.rem(x + dx, 4) * 2 + lax.rem(c + lax.rem(k, 2), 2)
         return (column * MSG + q).astype(F32), q
 
     def build(rows, m, out, g):
@@ -154,18 +155,21 @@
             build(rows, m, out, g)
             base = g * BLK
             send_block(g, out, dst, ssem, rsem, base, 1, 2048)
-            send_block(g + 4, out, dst, ssem, rsem, base, 1, 2048)
+            return 0
+
+        def again(g, _):
+            send_block(g + 4, out, dst, ssem, rsem, g * BLK, 1, 2048)
             return 0
 
         lax.fori_loop(0, 4, one, 0)
+        lax.fori_loop(0, 4, again, 0)
 
     dispatch(both, meta, msg, near, near_s, near_r)
 
     def clear(n, _):
         rows = pl.ds(pl.multiple_of(n * 256, 256), 256)
         for e in range(2):
-            ag[e, rows, :] = jnp.zeros((256, 256), F32)
-            au[e, rows, :] = jnp.zeros((256, 256), F32)
+            agu[e, rows, :] = jnp.zeros((256, 512), F32)
         return 0
 
     lax.fori_loop(0, 8, clear, 0)
@@ -186,19 +190,22 @@
         pltpu.make_async_remote_copy(block(near, k), block(above, k), fwd_s.at[1], above_r.at[k], device_id=down, device_id_type=MESH).start()
         return 0
 
-    def half(ref, h):
-        return ref.at[pl.ds(h * HALF, HALF)]
-
-    def load(buf, h):
-        return pltpu.make_async_copy(half(buf, h), stage, st_s.at[0])
+    def load(buf, h, b):
+        return pltpu.make_async_copy(
+            buf.at[pl.ds(pl.multiple_of(h * HALF + b * BLK, BLK), BLK)], stage.at[pl.ds(pl.multiple_of(b * BLK, BLK), BLK)], stage_s.at[b]
+        )
 
     def compute(buf, h, out):
-        cp = load(buf, h)
-        cp.start()
-        cp.wait()
+        for b in range(4):
+            load(buf, h, b).start()
 
         def sort_in(i, _):
             b, n = lax.div(i, 4), lax.rem(i, 4)
+
+            @pl.when(n == 0)
+            def _():
+                load(buf, h, b).wait()
+
             cols = pl.ds(pl.multiple_of(n * WIDE, WIDE), WIDE)
             v = dot(perm[...], stage[pl.ds(pl.multiple_of(b * BLK, BLK), BLK), cols], AT).astype(BF)
             rows = pl.ds(pl.multiple_of(b * MSG, MSG), MSG)
@@ -211,21 +218,20 @@
         lax.fori_loop(0, 16, sort_in, 0)
 
         def expert(e, _):
-            gate = dot(tok[e], wg[e], AT)
-            upv = dot(tok[e], wu[e], AT)
+            gate = dot(tok[e], wgu[e, :, 0:256], AT)
+            upv = dot(tok[e], wgu[e, :, 256:512], AT)
             hg = dot(grad[e], wd[e], TB)
             s = jax.nn.sigmoid(gate)
             silu = gate * s
-            hid[0] = (silu * upv).astype(BF)
-            hid[1] = (hg * upv * s * (1.0 + gate * (1.0 - s))).astype(BF)
-            hid[2] = (hg * silu).astype(BF)
+            act[...] = (silu * upv).astype(BF)
+            hid[:, 0:256] = (hg * upv * s * (1.0 + gate * (1.0 - s))).astype(BF)
+            hid[:, 256:512] = (hg * silu).astype(BF)
 
             def tile(n, _):
                 cols = pl.ds(pl.multiple_of(n * WIDE, WIDE), WIDE)
-                part[e, :, cols] = (dot(hid[1], wg[e, cols, :], TB) + dot(hid[2], wu[e, cols, :], TB)).astype(BF)
-                ag[e, cols, :] += dot(tok[e, :, cols], hid[1], TA)
-                au[e, cols, :] += dot(tok[e, :, cols], hid[2], TA)
-                ad[e, :, cols] += dot(hid[0], grad[e, :, cols], TA)
+                part[e, :, cols] = dot(hid[...], wgu[e, cols, :], TB).astype(BF)
+                agu[e, cols, :] += dot(tok[e, :, cols], hid[...], TA)
+                ad[e, :, cols] += dot(act[...], grad[e, :, cols], TA)
                 return 0
 
             lax.fori_loop(0, 2048 // WIDE, tile, 0)
@@ -251,97 +257,108 @@
 
         lax.fori_loop(4 * h, 4 * h + 4, one, 0)
 
-    def give(h):
-        def one(k, _):
-            pltpu.make_async_remote_copy(block(p_below, k), block(ret_a, k), ret_s.at[0], reta_r.at[k], device_id=down, device_id_type=MESH).start()
-            pltpu.make_async_remote_copy(block(p_above, k), block(ret_b, k), ret_s.at[1], retb_r.at[k], device_id=up, device_id_type=MESH).start()
-            return 0
-
-        lax.fori_loop(4 * h, 4 * h + 4, one, 0)
-
-    def settle(h):
-        def one(k, _):
-            got(ret_a, k, reta_r)
-            got(ret_b, k, retb_r)
-            ca = pltpu.make_async_copy(block(ret_a, k), rstage.at[pl.ds(0, BLK)], st_s.at[1])
-            cb = pltpu.make_async_copy(block(ret_b, k), rstage.at[pl.ds(BLK, BLK)], st_s.at[2])
-            ca.start()
-            cb.start()
-            ca.wait()
-            cb.wait()
-            rows = pl.ds(pl.multiple_of(k * BLK, BLK), BLK)
-            p_near[rows, :] = (p_near[rows, :].astype(F32) + rstage[0:BLK, :].astype(F32) + rstage[BLK : 2 * BLK, :].astype(F32)).astype(BF)
-            send_block(k, p_near, back, back_s, back_r, k * BLK, -1, 1024)
-            return 0
-
-        lax.fori_loop(4 * h, 4 * h + 4, one, 0)
-
-    def combine(buf, sem, m):
-        dacc[...] = jnp.zeros_like(dacc)
-
-        def one(k, _):
-            got(buf, k, sem)
-            cp = pltpu.make_async_copy(block(buf, k), rstage.at[pl.ds(0, BLK)], st_s.at[1])
-            cp.start()
-            want, q = rows_of(k)
-            t0, t1 = m[0:1, :], m[1:2, :]
-            lo = jnp.where(q < 24, jnp.where((want == t0) | (want == t1), 1.0, 0.0), 0.0).astype(BF)
-            hi = jnp.where(q >= 24, jnp.where((want - 24.0 == t0) | (want - 24.0 == t1), 1.0, 0.0), 0.0).astype(BF)
-            cp.wait()
-            dacc[:, 0:1024] += dot(lo, rstage[0:BLK, :], TA)
-            dacc[:, 1024:2048] += dot(hi, rstage[0:BLK, :], TA)
-            return 0
-
-        lax.fori_loop(0, 8, one, 0)
+    def give(k, _, buf=None, land=None, rsem=None, i=0, to=None):
+        pltpu.make_async_remote_copy(block(buf, k), block(land, k), ret_s.at[i], rsem.at[k], device_id=to, device_id_type=MESH).start()
+        return 0
+
+    def give_down(h):
+        lax.fori_loop(4 * h, 4 * h + 4, functools.partial(give, buf=p_below, land=ret_a, rsem=reta_r, i=0, to=down), 0)
+
+    def give_up(h):
+        lax.fori_loop(4 * h, 4 * h + 4, functools.partial(give, buf=p_above, land=ret_b, rsem=retb_r, i=1, to=up), 0)
+
+    def settle(k, _):
+        got(ret_a, k, reta_r)
+        got(ret_b, k, retb_r)
+        ca = pltpu.make_async_copy(block(ret_a, k), rstage.at[pl.ds(0, BLK)], st_s.at[0])
+        cb = pltpu.make_async_copy(block(ret_b, k), rstage.at[pl.ds(BLK, BLK)], st_s.at[1])
+        ca.start()
+        cb.start()
+        ca.wait()
+        cb.wait()
+        rows = pl.ds(pl.multiple_of(k * BLK, BLK), BLK)
+        p_near[rows, :] = (p_near[rows, :].astype(F32) + rstage[0:BLK, :].astype(F32) + rstage[BLK : 2 * BLK, :].astype(F32)).astype(BF)
+        send_block(k, p_near, back, back_s, back_r, k * BLK, -1, 1024)
+        return 0
+
+    def combine(k, _, buf=None, sem=None, m=None):
+        got(buf, k, sem)
+        cp = pltpu.make_async_copy(block(buf, k), rstage.at[pl.ds(0, BLK)], st_s.at[0])
+        cp.start()
+        want, q = rows_of(k)
+        t0, t1 = m[0:1, :], m[1:2, :]
+        lo = jnp.where(q < 24, jnp.where((want == t0) | (want == t1), 1.0, 0.0), 0.0).astype(BF)
+        hi = jnp.where(q >= 24, jnp.where((want - 24.0 == t0) | (want - 24.0 == t1), 1.0, 0.0), 0.0).astype(BF)
+        cp.wait()
+        dacc[:, 0:1024] += dot(lo, rstage[0:BLK, :], TA)
+        dacc[:, 1024:2048] += dot(hi, rstage[0:BLK, :], TA)
+        return 0
+
+    home = pltpu.make_async_remote_copy(dsend, dfar, dfar_s.at[0], dfar_r.at[0], device_id=over, device_id_type=MESH)
+    mine = functools.partial(combine, buf=back, sem=back_r, m=meta)
+    theirs = functools.partial(combine, buf=back_o, sem=backo_r, m=far_meta)
+
+    def send_opp(k, _):
+        send_block(k, p_opp, back_o, backo_s, backo_r, k * BLK, -1, 1024)
+        return 0
 
     lax.fori_loop(0, 4, forward, 0)
-    compute(near, 0, p_near)
-    lax.fori_loop(4, 8, forward, 0)
     for cp in fars:
         cp.wait()
     dispatch(far, far_meta, msg_o, opp, opp_s, opp_r)
+    compute(near, 0, p_near)
+    lax.fori_loop(4, 8, forward, 0)
     compute(near, 1, p_near)
 
     got_half(below, 0, below_r)
     compute(below, 0, p_below)
+    give_down(0)
     got_half(above, 0, above_r)
     compute(above, 0, p_above)
-    give(0)
-
-    def send_opp(k, _):
-        send_block(k, p_opp, back_o, backo_s, backo_r, k * BLK, -1, 1024)
-        return 0
-
-    for h in range(2):
-        got_half(opp, h, opp_r)
-        compute(opp, h, p_opp)
-        lax.fori_loop(4 * h, 4 * h + 4, send_opp, 0)
+    give_up(0)
+
+    got_half(opp, 0, opp_r)
+    compute(opp, 0, p_opp)
+    lax.fori_loop(0, 4, send_opp, 0)
 
     got_half(below, 1, below_r)
     compute(below, 1, p_below)
+    give_down(1)
     got_half(above, 1, above_r)
     compute(above, 1, p_above)
-    give(1)
+    give_up(1)
+
+    got_half(opp, 1, opp_r)
+    compute(opp, 1, p_opp)
+    lax.fori_loop(4, 8, send_opp, 0)
 
     outs = [
-        pltpu.make_async_copy(ag, gg_out, out_s.at[0]),
-        pltpu.make_async_copy(au, gu_out, out_s.at[1]),
+        pltpu.make_async_copy(agu.at[:, :, pl.ds(0, 256)], gg_out, out_s.at[0]),
+        pltpu.make_async_copy(agu.at[:, :, pl.ds(256, 256)], gu_out, out_s.at[1]),
         pltpu.make_async_copy(ad, gd_out, out_s.at[2]),
     ]
     for cp in outs:
         cp.start()
 
-    settle(0)
-    combine(back_o, backo_r, far_meta)
+    lax.fori_loop(0, 5, settle, 0)
+    dacc[...] = jnp.zeros_like(dacc)
+    lax.fori_loop(0, 8, theirs, 0)
     dsend[...] = dacc[...].astype(BF)
-    home = pltpu.make_async_remote_copy(dsend, dfar, dfar_s.at[0], dfar_r.at[0], device_id=over, device_id_type=MESH)
     home.start()
-    settle(1)
-    combine(back, back_r, meta)
+    dacc[...] = jnp.zeros_like(dacc)
+
+    def both_ways(k, _):
+        settle(k, 0)
+        mine(2 * k - 10, 0)
+        mine(2 * k - 9, 0)
+        return 0
+
+    lax.fori_loop(5, 7, both_ways, 0)
+    settle(7, 0)
+    lax.fori_loop(4, 8, mine, 0)
     home.wait()
-    dacc[...] = dacc[...] + dfar[...].astype(F32)
-    dsend[...] = dacc[...].astype(BF)
-    last = pltpu.make_async_copy(dsend, d_out, out_s.at[3])
+    dout[...] = (dacc[...] + dfar[...].astype(F32)).astype(BF)
+    last = pltpu.make_async_copy(dout, d_out, out_s.at[3])
     last.start()
 
     def sent(ref, rows, sem, i):
@@ -380,14 +397,14 @@
             pltpu.VMEM((256, 2048), BF), pltpu.VMEM((256, 2048), BF), pltpu.VMEM((8, 128), F32), pltpu.VMEM((8, 128), F32),
             pltpu.VMEM((4 * BLK, 2048), BF), pltpu.VMEM((4 * BLK, 2048), BF), pltpu.VMEM((BLK, BLK), BF),
             pltpu.VMEM((HALF, 2048), BF), pltpu.VMEM((2, BLK, 2048), BF), pltpu.VMEM((2, BLK, 2048), BF),
-            pltpu.VMEM((3, BLK, 256), BF), pltpu.VMEM((2, BLK, 2048), BF),
+            pltpu.VMEM((BLK, 256), BF), pltpu.VMEM((BLK, 512), BF), pltpu.VMEM((2, BLK, 2048), BF),
             pltpu.VMEM((ROWS, 1024), BF), pltpu.VMEM((ROWS, 1024), BF), pltpu.VMEM((ROWS, 1024), BF), pltpu.VMEM((ROWS, 1024), BF),
             pltpu.VMEM((2 * BLK, 1024), BF), pltpu.VMEM((128, 2048), F32), pltpu.VMEM((128, 2048), BF), pltpu.VMEM((128, 2048), BF),
-            pltpu.VMEM((2, 2048, 256), BF), pltpu.VMEM((2, 2048, 256), BF), pltpu.VMEM((2, 256, 2048), BF),
-            pltpu.VMEM((2, 2048, 256), F32), pltpu.VMEM((2, 2048, 256), F32), pltpu.VMEM((2, 256, 2048), F32),
+            pltpu.VMEM((2, 2048, 512), BF), pltpu.VMEM((2, 256, 2048), BF),
+            pltpu.VMEM((2, 2048, 512), F32), pltpu.VMEM((2, 256, 2048), F32), pltpu.VMEM((128, 2048), BF),
             dma((3,)), dma((3,)), dma((5,)), dma((1,)), dma((8,)), dma((1,)), dma((8,)), dma((2,)), dma((8,)), dma((8,)),
             dma((1,)), dma((2,)), dma((8,)), dma((8,)), dma((1,)), dma((8,)), dma((1,)), dma((8,)), dma((1,)), dma((1,)),
-            dma((3,)), dma((4,)),
+            dma((3,)), dma((4,)), dma((4,)),
         ],
         compiler_params=pltpu.CompilerParams(collective_id=0, has_side_effects=True, vmem_limit_bytes=62 * 2**20),
     )(tokens, out_grad, meta, wg, wu, wd)

time: 314 us -> 291 us (0.927)
  the two profiles are of different devices: /device:TPU:1 before, /device:TPU:97 now
where the time goes in v2:
time: 291 us; the launch traced here: 289 us
  Pallas kernels  274 us (94%)
  local copies, waits for them, and re-layouts  12.3 us (4%)
    pallas_call x1, Pallas kernels, body(): pl.pallas_call(kernel, name='expert_backward', out_shape=[sd((128, 2048),...  274 us
    unnamed x8, local copies, waits for them, and re-layouts  12.2 us

profile of v2, /device:TPU:97, one launch (start us, length us, event | category | flops | bytes accessed | tf_op | source)
XLA Modules:
  0.0 289.4 jit_solution(303157168526398903)
XLA Ops:
  0.6 0.1 pad.2.clone
  0.7 0.7 convert_bitcast_fusion
  1.4 1.3 maximum_maximum_fusion.meta_in
  2.7 274.4 %expert_backward.1 = (bf16[128,2048]{1,0:T(8,128)(2,1)}, f32[2,2048,256]{2,1,0:T(8,128)}, f32[2,2048,256]{2,1,0:T(8,128)}, f32[2,256,2048]{2,1,0:T(8,128)}, bf16...) custom-call(bf16[128,2048]{1,0:T(8,128)(2,1)} %tokens.1, ...), custom_call_target="tpu_custom_call" | custom-call | tf_op jit(solution)/shard_map/expert_backward/pallas_call | solution.py:387
  277.2 1.9 copy.15
  279.0 0.0 copy-start.1
  279.0 4.6 %copy.16 = f32[2,2048,256]{2,1,0:T(8,128)} copy(f32[2,2048,256]{2,1,0:T(8,128)} %get-tuple-element.17) | data formatting | bytes 8388608
  283.7 0.0 copy-done.1
  283.7 0.0 copy-start
  283.7 2.1 copy.17
  285.8 1.6 copy-done
  287.4 2.0 copy.18
  (1 shorter events, 0.0 us)
Async XLA Ops:
  279.0 4.6 %copy-start.1 = (f32[2,2048,256]{2,1,0:T(8,128)S(1)}, f32[2,2048,256]{2,1,0:T(8,128)}, u32[]{:S(2)}) copy-start(f32[2,2048,256]{2,1,0:T(8,128)} %get-tuple-element.18) | copy-start | bytes 12582916
  283.7 3.7 %copy-start = (f32[2,256,2048]{2,1,0:T(8,128)S(1)}, f32[2,256,2048]{2,1,0:T(8,128)}, u32[]{:S(2)}) copy-start(f32[2,256,2048]{2,1,0:T(8,128)} %get-tuple-element.19) | copy-start | bytes 12582916

commit v3 on v2

--- a/solution.py
+++ b/solution.py
@@ -36,24 +36,27 @@
 
 def kernel(
     tokens, out_grad, meta_in, wg_hbm, wu_hbm, wd_hbm,
-    d_out, gg_out, gu_out, gd_out, near, above, below, opp, ret_a, ret_b, back, back_o,
-    both, far, meta, far_meta, msg, msg_o, perm, stage, tok, grad, act, hid, part, p_near, p_above, p_below, p_opp,
-    rstage, dacc, dsend, dfar, wgu, wd, agu, ad, dout,
-    far_s, far_r, loc, near_s, near_r, opp_s, opp_r, fwd_s, above_r, below_r, pa_s, ret_s, reta_r, retb_r,
-    back_s, back_r, backo_s, backo_r, dfar_s, dfar_r, st_s, out_s, stage_s,
+    dout, agu, ad, near, above, below, opp, ret_a, ret_b, back, back_o,
+    raw, raw_o, meta, meta_o, msg, perm, stage, tok, grad, act, hid, part, p_near, p_above, p_below, p_opp,
+    rstage, dacc, dsend, dfar, wgu, wd,
+    far_s, far_r, loc, ys, yr, yms, ymr, yos, yor, yoms, yomr, near_s, near_r, opp_s, opp_r, fwd_s, above_r, below_r, pa_s, ret_s, reta_r, retb_r,
+    back_s, back_r, backo_s, backo_r, dfar_s, dfar_r, st_s, stage_s,
 ):
     x, y, z, c = place()
     up = device(x, y, lax.rem(z + 1, 4), c)
     down = device(x, y, lax.rem(z + 3, 4), c)
     over = device(x, y, lax.rem(z + 2, 4), c)
 
+    def hop(j):
+        return j + lax.div(j, 2) * (1 - 2 * lax.rem(j, 2))
+
     def peer(k, dx, sign):
-        dy, dc = lax.rem(lax.div(k, 2) + dx, 4), lax.rem(k, 2)
+        dy, dc = hop(lax.div(k, 2)), lax.rem(k, 2)
         return device(lax.rem(x + sign * dx + 4, 4), lax.rem(y + sign * dy + 4, 4), z, lax.rem(c + dc, 2))
 
     loads = [
-        pltpu.make_async_copy(tokens, both.at[pl.ds(0, 128)], loc.at[0]),
-        pltpu.make_async_copy(out_grad, both.at[pl.ds(128, 128)], loc.at[1]),
+        pltpu.make_async_copy(tokens, raw.at[0, pl.ds(0, 128)], loc.at[0]),
+        pltpu.make_async_copy(out_grad, raw.at[0, pl.ds(128, 128)], loc.at[1]),
         pltpu.make_async_copy(wg_hbm, wgu.at[:, :, pl.ds(0, 256)], loc.at[2]),
         pltpu.make_async_copy(wu_hbm, wgu.at[:, :, pl.ds(256, 256)], loc.at[3]),
         pltpu.make_async_copy(wd_hbm, wd, loc.at[4]),
@@ -82,34 +85,47 @@
         slot = jnp.sum(jnp.where(hit, earlier, 0.0), axis=0, keepdims=True)
         return 24.0 * e - 12.0 * (e - 2.0 * jnp.floor(e * 0.5)) + slot
 
-    meta[0:1, :] = row_of(h0, e0)
-    meta[1:2, :] = row_of(h1, e1)
-    meta[2:4, :] = meta_in[2:4, :]
-    meta[4:8, :] = meta_in[4:8, :]
+    meta[0, 0:1, :] = row_of(h0, e0)
+    meta[0, 1:2, :] = row_of(h1, e1)
+    meta[0, 2:8, :] = meta_in[2:8, :]
 
     ri = lax.broadcasted_iota(jnp.int32, (BLK, BLK), 0)
     ci = lax.broadcasted_iota(jnp.int32, (BLK, BLK), 1)
     src = lax.div(lax.rem(ri, MSG), CAP) * MSG + lax.div(ri, MSG) * CAP + lax.rem(ri, CAP)
     perm[...] = jnp.where(ci == src, 1.0, 0.0).astype(BF)
 
+    loads[0].wait()
+    loads[1].wait()
     pl.semaphore_wait(barrier, 34)
-    fars = [
-        pltpu.make_async_remote_copy(tokens, far.at[pl.ds(0, 128)], far_s.at[0], far_r.at[0], device_id=over, device_id_type=MESH),
-        pltpu.make_async_remote_copy(out_grad, far.at[pl.ds(128, 128)], far_s.at[1], far_r.at[1], device_id=over, device_id_type=MESH),
-        pltpu.make_async_remote_copy(meta, far_meta, far_s.at[2], far_r.at[2], device_id=over, device_id_type=MESH),
-    ]
+
+    def remote(a, b, ss, rs, to):
+        return pltpu.make_async_remote_copy(a, b, ss, rs, device_id=to, device_id_type=MESH)
+
+    def along_y(rows, m, rs, rr, ms, mr):
+        pairs = []
+        for j, dy in ((1, 1), (2, 3), (3, 2)):
+            to = device(x, lax.rem(y + dy, 4), z, c)
+            pairs.append((remote(rows.at[0], rows.at[j], rs.at[j], rr.at[j], to), remote(m.at[0], m.at[j], ms.at[j], mr.at[j], to)))
+        return pairs
+
+    fars = [remote(meta.at[0], meta_o.at[0], far_s.at[1], far_r.at[1], over), remote(raw.at[0], raw_o.at[0], far_s.at[0], far_r.at[0], over)]
+    sides = along_y(raw, meta, ys, yr, yms, ymr)
+    sides_o = along_y(raw_o, meta_o, yos, yor, yoms, yomr)
+    for a, b in sides:
+        b.start()
+        a.start()
     for cp in fars:
         cp.start()
 
-    def rows_of(k):
+    def rows_at(row, k):
         r = lax.broadcasted_iota(jnp.int32, (BLK, 1), 0)
         q, dx = lax.rem(r, MSG), lax.div(r, MSG)
-        column = lax.rem(y + lax.div(k, 2) + dx, 2) * 8 + lax.rem(x + dx, 4) * 2 + lax.rem(c + lax.rem(k, 2), 2)
+        column = lax.rem(row, 2) * 8 + lax.rem(x + dx, 4) * 2 + lax.rem(c + lax.rem(k, 2), 2)
         return (column * MSG + q).astype(F32), q
 
-    def build(rows, m, out, g):
-        want, q = rows_of(g)
-        t0, t1, p0, p1 = m[0:1, :], m[1:2, :], m[2:3, :], m[3:4, :]
+    def build(rows, m, j, g):
+        want, q = rows_at(y, g)
+        t0, t1, p0, p1 = m[j, 0:1, :], m[j, 1:2, :], m[j, 2:3, :], m[j, 3:4, :]
         hit_t = (want == t0) | (want == t1)
         hit0, hit1 = want - 24.0 == t0, want - 24.0 == t1
         hit_t = jnp.where(q < 24, jnp.where(hit_t, 1.0, 0.0), 0.0)
@@ -121,7 +137,7 @@
 
         def part_of(n, _):
             cols = pl.ds(pl.multiple_of(n * WIDE, WIDE), WIDE)
-            out[pl.ds(base, BLK), cols] = (dot(pick, rows[:, cols], AT) * scale).astype(BF)
+            msg[pl.ds(base, BLK), cols] = (dot(pick, rows[j, :, cols], AT) * scale).astype(BF)
             return 0
 
         lax.fori_loop(0, 2048 // WIDE, part_of, 0)
@@ -147,24 +163,56 @@
     def got(ref, k, sem):
         pltpu.make_async_copy(block(ref, k), block(ref, k), sem.at[k]).wait()
 
-    loads[0].wait()
-    loads[1].wait()
-
-    def dispatch(rows, m, out, dst, ssem, rsem):
-        def one(g, _):
-            build(rows, m, out, g)
-            base = g * BLK
-            send_block(g, out, dst, ssem, rsem, base, 1, 2048)
-            return 0
-
-        def again(g, _):
-            send_block(g + 4, out, dst, ssem, rsem, g * BLK, 1, 2048)
-            return 0
-
-        lax.fori_loop(0, 4, one, 0)
-        lax.fori_loop(0, 4, again, 0)
-
-    dispatch(both, meta, msg, near, near_s, near_r)
+    def leave(k, dst, ssem, rsem):
+        own = lax.rem(k, 2)
+        for dx in range(4):
+            at = pl.ds(pl.multiple_of(k * BLK + dx * MSG, MSG), MSG)
+            to = device(lax.rem(x + dx, 4), y, z, lax.rem(c + own, 2))
+            if dx == 0:
+                @pl.when(own == 0)
+                def _():
+                    pltpu.make_async_copy(msg.at[at], dst.at[at], rsem.at[k]).start()
+
+                @pl.when(own == 1)
+                def _():
+                    remote(msg.at[at], dst.at[at], ssem.at[k], rsem.at[k], to).start()
+            else:
+                remote(msg.at[at], dst.at[at], ssem.at[k], rsem.at[k], to).start()
+
+    def left(k, ssem):
+        three, one = near.at[pl.ds(0, 3 * MSG)], near.at[pl.ds(0, MSG)]
+        pltpu.make_async_copy(three, three, ssem.at[k]).wait()
+
+        @pl.when(lax.rem(k, 2) == 1)
+        def _():
+            pltpu.make_async_copy(one, one, ssem.at[k]).wait()
+
+    def dispatch(j):
+        if j:
+            sides[j - 1][0].wait_recv()
+            sides[j - 1][1].wait_recv()
+
+        def one(k, _):
+            build(raw, meta, j, k)
+            leave(k, near, near_s, near_r)
+            return 0
+
+        lax.fori_loop(2 * j, 2 * j + 2, one, 0)
+
+    def dispatch_o(j):
+        if j:
+            sides_o[j - 1][0].wait_recv()
+            sides_o[j - 1][1].wait_recv()
+
+        def one(k, _):
+            left(k, near_s)
+            build(raw_o, meta_o, j, k)
+            leave(k, opp, opp_s, opp_r)
+            return 0
+
+        lax.fori_loop(2 * j, 2 * j + 2, one, 0)
+
+    dispatch(0)
 
     def clear(n, _):
         rows = pl.ds(pl.multiple_of(n * 256, 256), 256)
@@ -285,8 +333,8 @@
         got(buf, k, sem)
         cp = pltpu.make_async_copy(block(buf, k), rstage.at[pl.ds(0, BLK)], st_s.at[0])
         cp.start()
-        want, q = rows_of(k)
-        t0, t1 = m[0:1, :], m[1:2, :]
+        want, q = rows_at(y + hop(lax.div(k, 2)), k)
+        t0, t1 = m[0, 0:1, :], m[0, 1:2, :]
         lo = jnp.where(q < 24, jnp.where((want == t0) | (want == t1), 1.0, 0.0), 0.0).astype(BF)
         hi = jnp.where(q >= 24, jnp.where((want - 24.0 == t0) | (want - 24.0 == t1), 1.0, 0.0), 0.0).astype(BF)
         cp.wait()
@@ -296,18 +344,29 @@
 
     home = pltpu.make_async_remote_copy(dsend, dfar, dfar_s.at[0], dfar_r.at[0], device_id=over, device_id_type=MESH)
     mine = functools.partial(combine, buf=back, sem=back_r, m=meta)
-    theirs = functools.partial(combine, buf=back_o, sem=backo_r, m=far_meta)
+    theirs = functools.partial(combine, buf=back_o, sem=backo_r, m=meta_o)
 
     def send_opp(k, _):
         send_block(k, p_opp, back_o, backo_s, backo_r, k * BLK, -1, 1024)
         return 0
 
-    lax.fori_loop(0, 4, forward, 0)
+    lax.fori_loop(0, 2, forward, 0)
+    dispatch(1)
+    dispatch(2)
     for cp in fars:
-        cp.wait()
-    dispatch(far, far_meta, msg_o, opp, opp_s, opp_r)
+        cp.wait_recv()
+    for a, b in sides_o:
+        b.start()
+        a.start()
+    dispatch(3)
+    lax.fori_loop(2, 4, forward, 0)
     compute(near, 0, p_near)
-    lax.fori_loop(4, 8, forward, 0)
+    lax.fori_loop(4, 6, forward, 0)
+    dispatch_o(0)
+    lax.fori_loop(6, 8, forward, 0)
+    dispatch_o(1)
+    dispatch_o(2)
+    dispatch_o(3)
     compute(near, 1, p_near)
 
     got_half(below, 0, below_r)
@@ -321,6 +380,10 @@
     compute(opp, 0, p_opp)
     lax.fori_loop(0, 4, send_opp, 0)
 
+    got_half(opp, 1, opp_r)
+    compute(opp, 1, p_opp)
+    lax.fori_loop(4, 8, send_opp, 0)
+
     got_half(below, 1, below_r)
     compute(below, 1, p_below)
     give_down(1)
@@ -328,19 +391,7 @@
     compute(above, 1, p_above)
     give_up(1)
 
-    got_half(opp, 1, opp_r)
-    compute(opp, 1, p_opp)
-    lax.fori_loop(4, 8, send_opp, 0)
-
-    outs = [
-        pltpu.make_async_copy(agu.at[:, :, pl.ds(0, 256)], gg_out, out_s.at[0]),
-        pltpu.make_async_copy(agu.at[:, :, pl.ds(256, 256)], gu_out, out_s.at[1]),
-        pltpu.make_async_copy(ad, gd_out, out_s.at[2]),
-    ]
-    for cp in outs:
-        cp.start()
-
-    lax.fori_loop(0, 5, settle, 0)
+    lax.fori_loop(0, 4, settle, 0)
     dacc[...] = jnp.zeros_like(dacc)
     lax.fori_loop(0, 8, theirs, 0)
     dsend[...] = dacc[...].astype(BF)
@@ -349,32 +400,35 @@
 
     def both_ways(k, _):
         settle(k, 0)
-        mine(2 * k - 10, 0)
-        mine(2 * k - 9, 0)
-        return 0
-
-    lax.fori_loop(5, 7, both_ways, 0)
-    settle(7, 0)
+        mine(2 * k - 8, 0)
+        mine(2 * k - 7, 0)
+        return 0
+
+    lax.fori_loop(4, 6, both_ways, 0)
+    lax.fori_loop(6, 8, settle, 0)
     lax.fori_loop(4, 8, mine, 0)
     home.wait()
     dout[...] = (dacc[...] + dfar[...].astype(F32)).astype(BF)
-    last = pltpu.make_async_copy(dout, d_out, out_s.at[3])
-    last.start()
 
     def sent(ref, rows, sem, i):
         pltpu.make_async_copy(ref.at[pl.ds(0, rows)], ref.at[pl.ds(0, rows)], sem.at[i]).wait()
 
-    sent(near, 31 * MSG, near_s, 0)
-    sent(opp, 31 * MSG, opp_s, 0)
+    def last_left(k, _):
+        left(k, opp_s)
+        return 0
+
+    lax.fori_loop(0, 8, last_left, 0)
+    for cp in fars:
+        cp.wait_send()
+    for a, b in sides + sides_o:
+        a.wait_send()
+        b.wait_send()
     sent(near, ROWS, fwd_s, 0)
     sent(near, ROWS, fwd_s, 1)
     sent(ret_a, ROWS, ret_s, 0)
     sent(ret_b, ROWS, ret_s, 1)
     sent(back, 31 * MSG, back_s, 0)
     sent(back_o, 31 * MSG, backo_s, 0)
-    for cp in outs:
-        cp.wait()
-    last.wait()
 
 
 def body(tokens, out_grad, probs, ids, wg, wu, wd):
@@ -388,27 +442,27 @@
         kernel,
         name="expert_backward",
         out_shape=[
-            sd((128, 2048), BF), sd((2, 2048, 256), F32), sd((2, 2048, 256), F32), sd((2, 256, 2048), F32),
+            pltpu.VMEM((128, 2048), BF), pltpu.VMEM((2, 2048, 512), F32), pltpu.VMEM((2, 256, 2048), F32),
             wide, wide, wide, wide, slim, slim, slim, slim,
         ],
         in_specs=[hbm, hbm, vm, hbm, hbm, hbm],
-        out_specs=[hbm] * 12,
+        out_specs=[vm] * 3 + [hbm] * 8,
         scratch_shapes=[
-            pltpu.VMEM((256, 2048), BF), pltpu.VMEM((256, 2048), BF), pltpu.VMEM((8, 128), F32), pltpu.VMEM((8, 128), F32),
-            pltpu.VMEM((4 * BLK, 2048), BF), pltpu.VMEM((4 * BLK, 2048), BF), pltpu.VMEM((BLK, BLK), BF),
+            pltpu.VMEM((4, 256, 2048), BF), pltpu.VMEM((4, 256, 2048), BF), pltpu.VMEM((4, 8, 128), F32), pltpu.VMEM((4, 8, 128), F32),
+            pltpu.VMEM((ROWS, 2048), BF), pltpu.VMEM((BLK, BLK), BF),
             pltpu.VMEM((HALF, 2048), BF), pltpu.VMEM((2, BLK, 2048), BF), pltpu.VMEM((2, BLK, 2048), BF),
             pltpu.VMEM((BLK, 256), BF), pltpu.VMEM((BLK, 512), BF), pltpu.VMEM((2, BLK, 2048), BF),
             pltpu.VMEM((ROWS, 1024), BF), pltpu.VMEM((ROWS, 1024), BF), pltpu.VMEM((ROWS, 1024), BF), pltpu.VMEM((ROWS, 1024), BF),
             pltpu.VMEM((2 * BLK, 1024), BF), pltpu.VMEM((128, 2048), F32), pltpu.VMEM((128, 2048), BF), pltpu.VMEM((128, 2048), BF),
             pltpu.VMEM((2, 2048, 512), BF), pltpu.VMEM((2, 256, 2048), BF),
-            pltpu.VMEM((2, 2048, 512), F32), pltpu.VMEM((2, 256, 2048), F32), pltpu.VMEM((128, 2048), BF),
-            dma((3,)), dma((3,)), dma((5,)), dma((1,)), dma((8,)), dma((1,)), dma((8,)), dma((2,)), dma((8,)), dma((8,)),
+            dma((2,)), dma((2,)), dma((5,)), *[dma((4,))] * 8, dma((8,)), dma((8,)), dma((8,)), dma((8,)), dma((2,)), dma((8,)), dma((8,)),
             dma((1,)), dma((2,)), dma((8,)), dma((8,)), dma((1,)), dma((8,)), dma((1,)), dma((8,)), dma((1,)), dma((1,)),
-            dma((3,)), dma((4,)), dma((4,)),
+            dma((3,)), dma((4,)),
         ],
-        compiler_params=pltpu.CompilerParams(collective_id=0, has_side_effects=True, vmem_limit_bytes=62 * 2**20),
+        compiler_params=pltpu.CompilerParams(collective_id=0, has_side_effects=True, vmem_limit_bytes=46 * 2**20),
     )(tokens, out_grad, meta, wg, wu, wd)
-    return tuple(outs[:4])
+    d, gu, gd = outs[:3]
+    return d, gu[:, :, :256], gu[:, :, 256:], gd
 
 
 def solution(mesh):

time: 291 us -> 267 us (0.918)
  the two profiles are of different devices: /device:TPU:97 before, /device:TPU:1 now
where the time goes in v3:
time: 267 us; the launch traced here: 266 us
  Pallas kernels  256 us (96%)
  local copies, waits for them, and re-layouts  7.08 us (3%)
    pallas_call x1, Pallas kernels, body(): pl.pallas_call(kernel, name='expert_backward', out_shape=[pltpu.VMEM((128...  256 us

profile of v3, /device:TPU:1, one launch (start us, length us, event | category | flops | bytes accessed | tf_op | source)
XLA Modules:
  0.0 265.6 jit_solution(8710172831110875812)
XLA Ops:
  0.6 0.1 pad.2.clone
  0.7 0.7 convert_bitcast_fusion
  1.4 1.3 maximum_maximum_fusion.meta_in
  2.7 255.8 %expert_backward.1 = (bf16[128,2048]{1,0:T(8,128)(2,1)S(1)}, f32[2,2048,512]{2,1,0:T(8,128)S(1)}, f32[2,256,2048]{2,1,0:T(8,128)S(1)}, bf16[1536,2048]{1,0:T(8,1...) custom-call(bf16[128,2048]{1,0:T(8,128)(2,1)} %tokens.1, ...), custom_call_target="tpu_custom_call" | custom-call | tf_op jit(solution)/shard_map/expert_backward/pallas_call | solution.py:441
  258.5 0.8 copy.13
  259.3 2.0 copy.14
  261.4 4.2 %fusion = (f32[2,2048,256]{2,1,0:T(8,128)}, f32[2,2048,256]{2,1,0:T(8,128)}) fusion(f32[2,2048,512]{2,1,0:T(8,128)S(1)} %get-tuple-element.8), kind=kLoop, calls=%fused_computation.2 | loop fusion | bytes 16777216 | tf_op jit(solution)/shard_map/slice | solution.py:465
  (1 shorter events, 0.0 us)

commit v4 on v3

--- a/solution.py
+++ b/solution.py
@@ -35,12 +35,12 @@
 
 
 def kernel(
-    tokens, out_grad, meta_in, wg_hbm, wu_hbm, wd_hbm,
+    tokens, out_grad, ids, probs, wg_hbm, wu_hbm, wd_hbm,
     dout, agu, ad, near, above, below, opp, ret_a, ret_b, back, back_o,
     raw, raw_o, meta, meta_o, msg, perm, stage, tok, grad, act, hid, part, p_near, p_above, p_below, p_opp,
     rstage, dacc, dsend, dfar, wgu, wd,
     far_s, far_r, loc, ys, yr, yms, ymr, yos, yor, yoms, yomr, near_s, near_r, opp_s, opp_r, fwd_s, above_r, below_r, pa_s, ret_s, reta_r, retb_r,
-    back_s, back_r, backo_s, backo_r, dfar_s, dfar_r, st_s, stage_s,
+    back_s, back_r, backo_s, backo_r, dfar_s, dfar_r, st_s, stage_s, side_s,
 ):
     x, y, z, c = place()
     up = device(x, y, lax.rem(z + 1, 4), c)
@@ -74,7 +74,7 @@
 
     lax.fori_loop(1, 32, greet, 0)
 
-    e0, e1 = meta_in[0:1, :], meta_in[1:2, :]
+    e0, e1 = ids[0:1, :].astype(F32), ids[1:2, :].astype(F32)
     ei = lax.broadcasted_iota(jnp.int32, (32, 128), 0).astype(F32)
     h0, h1 = ei == e0, ei == e1
     before = (lax.broadcasted_iota(jnp.int32, (128, 128), 0) < lax.broadcasted_iota(jnp.int32, (128, 128), 1))
@@ -87,7 +87,8 @@
 
     meta[0, 0:1, :] = row_of(h0, e0)
     meta[0, 1:2, :] = row_of(h1, e1)
-    meta[0, 2:8, :] = meta_in[2:8, :]
+    meta[0, 2:4, :] = probs[...]
+    meta[0, 4:8, :] = jnp.zeros((4, 128), F32)
 
     ri = lax.broadcasted_iota(jnp.int32, (BLK, BLK), 0)
     ci = lax.broadcasted_iota(jnp.int32, (BLK, BLK), 1)
@@ -238,6 +239,18 @@
         pltpu.make_async_remote_copy(block(near, k), block(above, k), fwd_s.at[1], above_r.at[k], device_id=down, device_id_type=MESH).start()
         return 0
 
+    across = device(x, lax.rem(y + 2, 4), z, c)
+
+    def relay(k):
+        got(below, k, below_r)
+        got(above, k, above_r)
+        remote(block(below, k), block(below, k + 6), side_s.at[0], below_r.at[k + 6], across).start()
+        remote(block(above, k), block(above, k + 6), side_s.at[1], above_r.at[k + 6], across).start()
+
+    def arrived(k, _):
+        got(near, k, near_r)
+        return 0
+
     def load(buf, h, b):
         return pltpu.make_async_copy(
             buf.at[pl.ds(pl.multiple_of(h * HALF + b * BLK, BLK), BLK)], stage.at[pl.ds(pl.multiple_of(b * BLK, BLK), BLK)], stage_s.at[b]
@@ -298,12 +311,12 @@
 
         lax.fori_loop(0, 8, sort_out, 0)
 
-    def got_half(ref, h, sem):
+    def got_half(ref, h, sem, first=0):
         def one(k, _):
             got(ref, k, sem)
             return 0
 
-        lax.fori_loop(4 * h, 4 * h + 4, one, 0)
+        lax.fori_loop(4 * h + first, 4 * h + 4, one, 0)
 
     def give(k, _, buf=None, land=None, rsem=None, i=0, to=None):
         pltpu.make_async_remote_copy(block(buf, k), block(land, k), ret_s.at[i], rsem.at[k], device_id=to, device_id_type=MESH).start()
@@ -361,20 +374,20 @@
     dispatch(3)
     lax.fori_loop(2, 4, forward, 0)
     compute(near, 0, p_near)
+    relay(0)
     lax.fori_loop(4, 6, forward, 0)
     dispatch_o(0)
-    lax.fori_loop(6, 8, forward, 0)
+    relay(1)
+    lax.fori_loop(6, 8, arrived, 0)
     dispatch_o(1)
     dispatch_o(2)
     dispatch_o(3)
     compute(near, 1, p_near)
 
-    got_half(below, 0, below_r)
+    got_half(below, 0, below_r, 2)
     compute(below, 0, p_below)
-    give_down(0)
-    got_half(above, 0, above_r)
+    got_half(above, 0, above_r, 2)
     compute(above, 0, p_above)
-    give_up(0)
 
     got_half(opp, 0, opp_r)
     compute(opp, 0, p_opp)
@@ -383,6 +396,8 @@
     got_half(opp, 1, opp_r)
     compute(opp, 1, p_opp)
     lax.fori_loop(4, 8, send_opp, 0)
+    give_down(0)
+    give_up(0)
 
     got_half(below, 1, below_r)
     compute(below, 1, p_below)
@@ -423,8 +438,10 @@
     for a, b in sides + sides_o:
         a.wait_send()
         b.wait_send()
-    sent(near, ROWS, fwd_s, 0)
-    sent(near, ROWS, fwd_s, 1)
+    sent(near, 6 * BLK, fwd_s, 0)
+    sent(near, 6 * BLK, fwd_s, 1)
+    sent(near, 2 * BLK, side_s, 0)
+    sent(near, 2 * BLK, side_s, 1)
     sent(ret_a, ROWS, ret_s, 0)
     sent(ret_b, ROWS, ret_s, 1)
     sent(back, 31 * MSG, back_s, 0)
@@ -432,7 +449,6 @@
 
 
 def body(tokens, out_grad, probs, ids, wg, wu, wd):
-    meta = jnp.concatenate([ids.T.astype(F32), probs.T, jnp.zeros((4, 128), F32)], axis=0)
     hbm = pl.BlockSpec(memory_space=pltpu.HBM)
     vm = pl.BlockSpec(memory_space=pltpu.VMEM)
     sd = jax.ShapeDtypeStruct
@@ -445,7 +461,7 @@
             pltpu.VMEM((128, 2048), BF), pltpu.VMEM((2, 2048, 512), F32), pltpu.VMEM((2, 256, 2048), F32),
             wide, wide, wide, wide, slim, slim, slim, slim,
         ],
-        in_specs=[hbm, hbm, vm, hbm, hbm, hbm],
+        in_specs=[hbm, hbm, vm, vm, hbm, hbm, hbm],
         out_specs=[vm] * 3 + [hbm] * 8,
         scratch_shapes=[
             pltpu.VMEM((4, 256, 2048), BF), pltpu.VMEM((4, 256, 2048), BF), pltpu.VMEM((4, 8, 128), F32), pltpu.VMEM((4, 8, 128), F32),
@@ -457,10 +473,10 @@
             pltpu.VMEM((2, 2048, 512), BF), pltpu.VMEM((2, 256, 2048), BF),
             dma((2,)), dma((2,)), dma((5,)), *[dma((4,))] * 8, dma((8,)), dma((8,)), dma((8,)), dma((8,)), dma((2,)), dma((8,)), dma((8,)),
             dma((1,)), dma((2,)), dma((8,)), dma((8,)), dma((1,)), dma((8,)), dma((1,)), dma((8,)), dma((1,)), dma((1,)),
-            dma((3,)), dma((4,)),
+            dma((3,)), dma((4,)), dma((2,)),
         ],
         compiler_params=pltpu.CompilerParams(collective_id=0, has_side_effects=True, vmem_limit_bytes=46 * 2**20),
-    )(tokens, out_grad, meta, wg, wu, wd)
+    )(tokens, out_grad, ids.T, probs.T, wg, wu, wd)
     d, gu, gd = outs[:3]
     return d, gu[:, :, :256], gu[:, :, 256:], gd
 

time: 267 us -> 271 us (1.015)
  Pallas kernels: 256 us -> 262 us
    pallas_call x1, Pallas kernels: 256 us -> 262 us  [body(): pl.pallas_call(kernel, name='expert_backward', out_shape=[pltpu.VMEM((128...]
where the time goes in v4:
time: 271 us; the launch traced here: 270 us
  Pallas kernels  262 us (97%)
  local copies, waits for them, and re-layouts  7.01 us (3%)
    pallas_call x1, Pallas kernels, body(): pl.pallas_call(kernel, name='expert_backward', out_shape=[pltpu.VMEM((128...  262 us

profile of v4, /device:TPU:1, one launch (start us, length us, event | category | flops | bytes accessed | tf_op | source)
XLA Modules:
  0.0 269.6 jit_solution(4716079455706340113)
XLA Ops:
  0.6 262.0 %expert_backward.1 = (bf16[128,2048]{1,0:T(8,128)(2,1)S(1)}, f32[2,2048,512]{2,1,0:T(8,128)S(1)}, f32[2,256,2048]{2,1,0:T(8,128)S(1)}, bf16[1536,2048]{1,0:T(8,1...) custom-call(bf16[128,2048]{1,0:T(8,128)(2,1)} %tokens.1, ...), custom_call_target="tpu_custom_call" | custom-call | tf_op jit(solution)/shard_map/expert_backward/pallas_call | solution.py:457
  262.6 0.8 copy.13
  263.4 2.0 copy.14
  265.4 4.2 %fusion = (f32[2,2048,256]{2,1,0:T(8,128)}, f32[2,2048,256]{2,1,0:T(8,128)}) fusion(f32[2,2048,512]{2,1,0:T(8,128)S(1)} %get-tuple-element.8), kind=kLoop, calls=%fused_computation | loop fusion | bytes 16777216 | tf_op jit(solution)/shard_map/slice | solution.py:481
